TPU v7x, 1024 devices: a whole 8x8x8 slice. The times are simulated.
1024 devices in a mesh: grp: 8 (over y), reg: 128 (over z, x, core).
Axes of the slice: x: 8, y: 8, z: 8, core: 2. Of those that a mesh axis runs over, the one named last changes fastest.
Arguments:
- field: bfloat16 [128, 1024, 1024], P(None, 'reg', 'grp'), may hold values from -6 to 6
- send_pick: int32 [16384], P(('grp', 'reg')), may hold values from 0 to 7
- blk_src: int32 [32768], P(('grp', 'reg')), may hold values from 0 to 47, as said below
- blk_ocn: int32 [32768], P(('grp', 'reg')), may hold values from 0 to 4, as said below
- blk_weight: bfloat16 [32768, 384, 128], P(('grp', 'reg')), may hold values from -0.3125 to 0.3125
Outputs:
- remapped: bfloat16 [128, 524288], P(None, ('grp', 'reg'))
Inputs may be any that keep to these rules, and one draw needn't show every extreme that they name: `blk_src`: slots 0 to 15 are the lower region's pool, the next 16 the device's own, the last 16 the upper region's. Each device's blocks name at most 4 distinct slots of each neighbouring region's pool, exactly 4 on every device. `blk_ocn`: the value 4 marks an empty slot; every device has one or more empty slots.
All inputs are finite; a program needn't handle non-finite values.
Results may differ from a plain program's by a relative error of at most 0.0041.
Values may be sent and summed in bfloat16 or wider, within the bound.
A program may use at most 32 MiB of HBM per device.

v0:
```python
import jax
import jax.numpy as jnp
from jax import lax
from jax.sharding import PartitionSpec as P

OCN = 4


def padded(x, sides, width):
    for axis, dim in sides:
        devices, length = (lax.axis_size(axis), x.shape[dim])
        up = [(i, (i + 1) % devices) for i in range(devices - 1)]
        down = [(j, i) for i, j in up]
        last = lax.slice_in_dim(x, length - width, length, axis=dim)
        leading = lax.slice_in_dim(x, 0, width, axis=dim)
        before = lax.ppermute(last, axis, up)
        after = lax.ppermute(leading, axis, down)
        x = jnp.concatenate([before, x, after], axis=dim)
    return x


def per_device(field, send_pick, blk_src, blk_ocn, blk_weight):
    channels, rows, cells = field.shape
    wide = padded(field, (("grp", 2), ("reg", 1)), 1).astype(jnp.float32)
    grad_x = ((wide[:, 2:, 1:-1] - wide[:, :-2, 1:-1]) * 0.5).astype(jnp.bfloat16)
    groups = lax.axis_size("grp")
    pool_size = send_pick.shape[0]
    per_peer = pool_size // groups
    grad_y = ((wide[:, 1:-1, 2:] - wide[:, 1:-1, :-2]) * 0.5).astype(jnp.bfloat16)
    stacked = jnp.concatenate([field, grad_x, grad_y], axis=2)
    outgoing = jnp.take(stacked, send_pick, axis=1).reshape(channels, groups, per_peer, 3 * cells)
    received = lax.all_to_all(outgoing, "grp", split_axis=1, concat_axis=1, tiled=True)
    pool = received.reshape(channels, pool_size, 3 * cells)
    extended = padded(pool, (("reg", 1),), pool_size)
    sources = jnp.take(extended, blk_src, axis=1)
    partial_value = jnp.einsum(
        "cbs,bst->bct", sources, blk_weight, preferred_element_type=jnp.float32
    )
    onehot = (blk_ocn[None, :] == jnp.arange(OCN, dtype=jnp.int32)[:, None]).astype(jnp.float32)
    summed = jnp.einsum("ob,bct->cot", onehot, partial_value, precision=lax.Precision.HIGHEST)
    return summed.reshape(channels, OCN * cells).astype(jnp.bfloat16)


def solution(mesh):
    placed = (
        P(None, "reg", "grp"),
        P(("grp", "reg")),
        P(("grp", "reg")),
        P(("grp", "reg")),
        P(("grp", "reg"), None, None),
    )
    return jax.shard_map(
        per_device, mesh=mesh, in_specs=placed, out_specs=P(None, ("grp", "reg")), check_vma=False
    )
```

profile of v0, /device:TPU:399, one launch (start us, length us, event | category | flops | bytes accessed | tf_op | source)
XLA Modules:
  0.0 124.2 jit_solution(12771575609600523926)
XLA Ops:
  0.0 1.1 copy.9
  1.3 3.3 %collective-permute-start = (bf16[128,8,1]{2,0,1:T(8,128)(2,1)S(1)}, bf16[128,8,1]{2,0,1:T(8,128)(2,1)S(1)}, u32[]{:S(2)}, u32[]{:S(2)}) collective-permute-start(bf16[128,8,1]{2,0,1:T(8,128)(2,1)S(1)} %get-tuple-element.9), channel_id=1, source_target_pairs={{0,128},{128,256},{256,384},{384,512},{512,640},{640,768},{768,896... | collective-permute-start | bytes 6152 | tf_op jit(solution)/shard_map/ppermute | solution.py:16
  4.6 1.3 %collective-permute-start.1 = (bf16[128,8,1]{2,0,1:T(8,128)(2,1)S(1)}, bf16[128,8,1]{2,0,1:T(8,128)(2,1)S(1)}, u32[]{:S(2)}, u32[]{:S(2)}) collective-permute-start(bf16[128,8,1]{2,0,1:T(8,128)(2,1)S(1)} %get-tuple-element.10), channel_id=1, source_target_pairs={{128,0},{256,128},{384,256},{512,384},{640,512},{768,640},{896,768... | collective-permute-start | bytes 6152 | tf_op jit(solution)/shard_map/ppermute | solution.py:17
  6.0 3.6 %collective-permute-done = bf16[128,8,1]{2,0,1:T(8,128)(2,1)S(1)} collective-permute-done((bf16[128,8,1]{2,0,1:T(8,128)(2,1)S(1)}, bf16[128,8,1]{2,0,1:T(8,128)(2,1)S(1)}, u32[]{:S(2)}, u32[]{:S(2)}) %collective-permute-start) | collective-permute-done | bytes 2080 | tf_op jit(solution)/shard_map/ppermute | solution.py:16
  9.6 3.8 %collective-permute-done.1 = bf16[128,8,1]{2,0,1:T(8,128)(2,1)S(1)} collective-permute-done((bf16[128,8,1]{2,0,1:T(8,128)(2,1)S(1)}, bf16[128,8,1]{2,0,1:T(8,128)(2,1)S(1)}, u32[]{:S(2)}, u32[]{:S(2)}) %collective-permute-start.1) | collective-permute-done | bytes 2080 | tf_op jit(solution)/shard_map/ppermute | solution.py:17
  13.5 0.6 copy-done.2
  14.1 7.7 %collective-permute-start.2 = (bf16[128,1,130]{2,0,1:T(8,128)(2,1)S(1)}, bf16[128,1,130]{2,0,1:T(8,128)(2,1)}, u32[]{:S(2)}, u32[]{:S(2)}) collective-permute-start(bf16[128,1,130]{2,0,1:T(8,128)(2,1)S(1)} %get-tuple-element.7), channel_id=1, source_target_pairs={{0,1},{1,2},{2,3},{3,4},{4,5},{5,6},{6,7},{7,8},{8,9},{9,10},{10,1... | collective-permute-start | bytes 99848 | tf_op jit(solution)/shard_map/ppermute | solution.py:16
  21.8 1.9 %collective-permute-start.3 = (bf16[128,1,130]{2,0,1:T(8,128)(2,1)S(1)}, bf16[128,1,130]{2,0,1:T(8,128)(2,1)}, u32[]{:S(2)}, u32[]{:S(2)}) collective-permute-start(bf16[128,1,130]{2,0,1:T(8,128)(2,1)S(1)} %get-tuple-element.8), channel_id=1, source_target_pairs={{1,0},{2,1},{3,2},{4,3},{5,4},{6,5},{7,6},{8,7},{9,8},{10,9},{11,1... | collective-permute-start | bytes 99848 | tf_op jit(solution)/shard_map/ppermute | solution.py:17
  23.8 7.0 %collective-permute-done.3 = bf16[128,1,130]{2,0,1:T(8,128)(2,1)} collective-permute-done((bf16[128,1,130]{2,0,1:T(8,128)(2,1)S(1)}, bf16[128,1,130]{2,0,1:T(8,128)(2,1)}, u32[]{:S(2)}, u32[]{:S(2)}) %collective-permute-start.3) | collective-permute-done | bytes 33312 | tf_op jit(solution)/shard_map/ppermute | solution.py:17
  30.8 1.4 %maximum_convert_fusion = f32[128,10,130]{2,0,1:T(8,128)S(1)} fusion(bf16[128,1,130]{2,0,1:T(8,128)(2,1)} %collective-permute-done.3, bf16[128,8,1]{2,0,1:T(8,128)(2,1)} %copy-done.2, bf16[128,8,128]{2,0,1:T(8,128)(2,1)S(1)} %copy.9, bf16[128,8,1]{2,0,1:T(8,128)(2,1)} %copy-done.1, bf16[128,1,130]{2,0,1:T(8,128)(2,1)} %collective-permute-done.2), kind=kLoop, calls=%fused_computation.13 | loop fusion | flops 1664000 | bytes 998400 | tf_op jit(solution)/shard_map/convert_element_type | solution.py:24
  32.2 0.5 fusion.13
  32.6 1.0 pad_maximum_fusion.1
  33.6 3.1 %gather_fusion = bf16[16,128,384]{2,1,0:T(8,128)(2,1)} fusion(bf16[128,8,384]{2,0,1:T(8,128)(2,1)} %pad_maximum_fusion.1, s32[1024]{0:T(1024)S(1)} %pad_clamp_fusion.1), kind=kCustom, calls=%fused_computation | custom fusion | bytes 3145792 | tf_op jit(solution)/shard_map/jit(_take)/gather | solution.py:31
  36.7 1.6 %broadcast_select_fusion = bf16[128,8,2,384]{3,0,2,1:T(8,128)(2,1)S(1)} fusion(bf16[128,8,2,384]{3,0,2,1:T(8,128)(2,1)} %bitcast.19, pred[8,2]{1,0:T(8,128)(4,1)S(1)} %broadcast_in_dim.29), kind=kLoop, calls=%fused_computation.10 | loop fusion | flops 786432 | bytes 3145744 | tf_op jit(solution)/shard_map/jit(_take)/select_n | solution.py:31
  38.4 42.4 %all_to_all.5 = bf16[128,8,2,384]{3,0,2,1:T(8,128)(2,1)S(1)} all-to-all(bf16[128,8,2,384]{3,0,2,1:T(8,128)(2,1)S(1)} %broadcast_select_fusion), channel_id=1, replica_groups=mesh['grp'=8,'reg'=128] {'grp'}, dimensions={1} | all-to-all | bytes 3145728 | tf_op jit(solution)/shard_map/all_to_all | solution.py:32
  80.8 5.3 %collective-permute-start.4 = (bf16[128,16,384]{2,0,1:T(8,128)(2,1)S(1)}, bf16[128,16,384]{2,0,1:T(8,128)(2,1)S(1)}, u32[]{:S(2)}, u32[]{:S(2)}) collective-permute-start(bf16[128,16,384]{2,0,1:T(8,128)(2,1)S(1)} %bitcast.16), channel_id=1, source_target_pairs={{0,1},{1,2},{2,3},{3,4},{4,5},{5,6},{6,7},{7,8},{8,9},{9,10},{10,1... | collective-permute-start | bytes 4718600 | tf_op jit(solution)/shard_map/ppermute | solution.py:16
  86.1 1.9 %collective-permute-start.5 = (bf16[128,16,384]{2,0,1:T(8,128)(2,1)S(1)}, bf16[128,16,384]{2,0,1:T(8,128)(2,1)S(1)}, u32[]{:S(2)}, u32[]{:S(2)}) collective-permute-start(bf16[128,16,384]{2,0,1:T(8,128)(2,1)S(1)} %bitcast.17), channel_id=1, source_target_pairs={{1,0},{2,1},{3,2},{4,3},{5,4},{6,5},{7,6},{8,7},{9,8},{10,9},{11,1... | collective-permute-start | bytes 4718600 | tf_op jit(solution)/shard_map/ppermute | solution.py:17
  88.1 15.4 %collective-permute-done.4 = bf16[128,16,384]{2,0,1:T(8,128)(2,1)S(1)} collective-permute-done((bf16[128,16,384]{2,0,1:T(8,128)(2,1)S(1)}, bf16[128,16,384]{2,0,1:T(8,128)(2,1)S(1)}, u32[]{:S(2)}, u32[]{:S(2)}) %collective-permute-start.4) | collective-permute-done | bytes 1572896 | tf_op jit(solution)/shard_map/ppermute | solution.py:16
  103.5 7.7 %collective-permute-done.5 = bf16[128,16,384]{2,0,1:T(8,128)(2,1)S(1)} collective-permute-done((bf16[128,16,384]{2,0,1:T(8,128)(2,1)S(1)}, bf16[128,16,384]{2,0,1:T(8,128)(2,1)S(1)}, u32[]{:S(2)}, u32[]{:S(2)}) %collective-permute-start.5) | collective-permute-done | bytes 1572896 | tf_op jit(solution)/shard_map/ppermute | solution.py:17
  111.2 2.5 %pad_maximum_fusion = bf16[128,48,384]{2,0,1:T(8,128)(2,1)} fusion(bf16[128,16,384]{2,0,1:T(8,128)(2,1)S(1)} %collective-permute-done.5, bf16[128,16,384]{2,0,1:T(8,128)(2,1)S(1)} %bitcast.18, bf16[128,16,384]{2,0,1:T(8,128)(2,1)S(1)} %collective-permute-done.4), kind=kLoop, calls=%fused_computation.2 | loop fusion | flops 4718592 | bytes 9437184 | tf_op jit(solution)/shard_map/concatenate | solution.py:18
  113.6 5.0 %gather_fusion.1 = bf16[32,128,384]{2,1,0:T(8,128)(2,1)} fusion(bf16[128,48,384]{2,0,1:T(8,128)(2,1)} %pad_maximum_fusion, s32[1024]{0:T(1024)S(1)} %pad_clamp_fusion), kind=kCustom, calls=%fused_computation.1 | custom fusion | bytes 6291584 | tf_op jit(solution)/shard_map/jit(_take)/gather | solution.py:35
  118.6 3.0 %fusion = f32[32,128,128]{2,1,0:T(8,128)S(1)} fusion(bf16[32,384,128]{2,1,0:T(8,128)(2,1)S(1)} %copy-done, bf16[32,128,384]{2,1,0:T(8,128)(2,1)} %gather_fusion.1, pred[32]{0:T(512)(128)(4,1)S(1)} %compare_and_fusion.1), kind=kOutput, calls=%fused_computation.3 | convolution fusion | flops 404226048 | bytes 8388640 | tf_op jit(solution)/shard_map/cbs,bst->bct/dot_general | solution.py:36
  121.6 2.0 %fusion.7 = bf16[128,128,4]{1,2,0:T(4,128)(2,1)S(1)} fusion(f32[32,128,128]{2,1,0:T(8,128)S(1)} %fusion, s32[32]{0:T(128)S(1)} %copy-done.3), kind=kOutput, calls=%fused_computation.11 | convolution fusion | flops 25231488 | bytes 2228352 | tf_op jit(solution)/shard_map/ob,bct->cot/dot_general | solution.py:40
  123.5 0.7 copy.17
  (21 shorter events, 0.4 us)
Async XLA Ops:
  0.0 118.6 %copy-start = (bf16[32,384,128]{2,1,0:T(8,128)(2,1)S(1)}, bf16[32,384,128]{2,1,0:T(8,128)(2,1)}, u32[]{:S(2)}) copy-start(bf16[32,384,128]{2,1,0:T(8,128)(2,1)} %param.9) | copy-start | bytes 9437188
  0.0 5.9 %copy-start.4 = (s32[16]{0:T(128)S(1)}, s32[16]{0:T(128)}, u32[]{:S(2)}) copy-start(s32[16]{0:T(128)} %param.6) | copy-start | bytes 196
  1.3 8.3 %collective-permute-start = (bf16[128,8,1]{2,0,1:T(8,128)(2,1)S(1)}, bf16[128,8,1]{2,0,1:T(8,128)(2,1)S(1)}, u32[]{:S(2)}, u32[]{:S(2)}) collective-permute-start(bf16[128,8,1]{2,0,1:T(8,128)(2,1)S(1)} %get-tuple-element.9), channel_id=1, source_target_pairs={{0,128},{128,256},{256,384},{384,512},{512,640},{640,768},{768,896... | collective-permute-start | bytes 6152 | tf_op jit(solution)/shard_map/ppermute | solution.py:16
  4.6 8.8 %collective-permute-start.1 = (bf16[128,8,1]{2,0,1:T(8,128)(2,1)S(1)}, bf16[128,8,1]{2,0,1:T(8,128)(2,1)S(1)}, u32[]{:S(2)}, u32[]{:S(2)}) collective-permute-start(bf16[128,8,1]{2,0,1:T(8,128)(2,1)S(1)} %get-tuple-element.10), channel_id=1, source_target_pairs={{128,0},{256,128},{384,256},{512,384},{640,512},{768,640},{896,768... | collective-permute-start | bytes 6152 | tf_op jit(solution)/shard_map/ppermute | solution.py:17
  9.6 3.8 %copy-start.1 = (bf16[128,8,1]{2,0,1:T(8,128)(2,1)}, bf16[128,8,1]{2,0,1:T(8,128)(2,1)S(1)}, u32[]{:S(2)}) copy-start(bf16[128,8,1]{2,0,1:T(8,128)(2,1)S(1)} %collective-permute-done) | copy-start | bytes 6148
  13.4 0.7 copy-start.2
  14.1 9.7 %collective-permute-start.2 = (bf16[128,1,130]{2,0,1:T(8,128)(2,1)S(1)}, bf16[128,1,130]{2,0,1:T(8,128)(2,1)}, u32[]{:S(2)}, u32[]{:S(2)}) collective-permute-start(bf16[128,1,130]{2,0,1:T(8,128)(2,1)S(1)} %get-tuple-element.7), channel_id=1, source_target_pairs={{0,1},{1,2},{2,3},{3,4},{4,5},{5,6},{6,7},{7,8},{8,9},{9,10},{10,1... | collective-permute-start | bytes 99848 | tf_op jit(solution)/shard_map/ppermute | solution.py:16
  21.8 9.0 %collective-permute-start.3 = (bf16[128,1,130]{2,0,1:T(8,128)(2,1)S(1)}, bf16[128,1,130]{2,0,1:T(8,128)(2,1)}, u32[]{:S(2)}, u32[]{:S(2)}) collective-permute-start(bf16[128,1,130]{2,0,1:T(8,128)(2,1)S(1)} %get-tuple-element.8), channel_id=1, source_target_pairs={{1,0},{2,1},{3,2},{4,3},{5,4},{6,5},{7,6},{8,7},{9,8},{10,9},{11,1... | collective-permute-start | bytes 99848 | tf_op jit(solution)/shard_map/ppermute | solution.py:17
  38.4 49.7 %copy-start.5 = (s32[32]{0:T(128)S(1)}, s32[32]{0:T(128)}, u32[]{:S(2)}) copy-start(s32[32]{0:T(128)} %param.7) | copy-start | bytes 388
  80.8 22.7 %collective-permute-start.4 = (bf16[128,16,384]{2,0,1:T(8,128)(2,1)S(1)}, bf16[128,16,384]{2,0,1:T(8,128)(2,1)S(1)}, u32[]{:S(2)}, u32[]{:S(2)}) collective-permute-start(bf16[128,16,384]{2,0,1:T(8,128)(2,1)S(1)} %bitcast.16), channel_id=1, source_target_pairs={{0,1},{1,2},{2,3},{3,4},{4,5},{5,6},{6,7},{7,8},{8,9},{9,10},{10,1... | collective-permute-start | bytes 4718600 | tf_op jit(solution)/shard_map/ppermute | solution.py:16
  86.1 25.1 %collective-permute-start.5 = (bf16[128,16,384]{2,0,1:T(8,128)(2,1)S(1)}, bf16[128,16,384]{2,0,1:T(8,128)(2,1)S(1)}, u32[]{:S(2)}, u32[]{:S(2)}) collective-permute-start(bf16[128,16,384]{2,0,1:T(8,128)(2,1)S(1)} %bitcast.17), channel_id=1, source_target_pairs={{1,0},{2,1},{3,2},{4,3},{5,4},{6,5},{7,6},{8,7},{9,8},{10,9},{11,1... | collective-permute-start | bytes 4718600 | tf_op jit(solution)/shard_map/ppermute | solution.py:17
  118.6 3.0 %copy-start.3 = (s32[32]{0:T(128)S(1)}, s32[32]{0:T(128)}, u32[]{:S(2)}) copy-start(s32[32]{0:T(128)} %param.8) | copy-start | bytes 388
where the time goes:
time: 125 us; the launch traced here: 124 us
  blocking collectives  42.4 us (34%)
  waiting for transfers between devices  37.5 us (30%)
  starting transfers between devices  21.4 us (17%)
  local copies, waits for them, and re-layouts  10.7 us (9%)
  other arithmetic  7.1 us (6%)
  matrix products  4.92 us (4%)
    all_to_all x1, blocking collectives, per_device(): lax.all_to_all(outgoing, 'grp', split_axis=1, concat_axis=1, tiled=True)  42.4 us
    ppermute x3, waiting for transfers between devices, padded(): before = lax.ppermute(last, axis, up)  19 us
    ppermute x3, waiting for transfers between devices, padded(): after = lax.ppermute(leading, axis, down)  18.5 us
    ppermute x3, starting transfers between devices, padded(): before = lax.ppermute(last, axis, up)  16.3 us
    ppermute x3, starting transfers between devices, padded(): after = lax.ppermute(leading, axis, down)  5.13 us
    gather x1, local copies, waits for them, and re-layouts, per_device(): sources = jnp.take(extended, blk_src, axis=1)  4.95 us
    gather x1, local copies, waits for them, and re-layouts, per_device(): jnp.take(stacked, send_pick, axis=1)  3.06 us
    dot_general x1, matrix products, per_device(): jnp.einsum('cbs,bst->bct', sources, blk_weight, preferred_element_type=jn...  2.96 us
  transfers between devices with their start and end apart: 6, of which 5 were waited for; matrix products, arithmetic and copies ran while one was open for 0% of the time, Pallas kernels for 0%

commit v1 on v0

v1 whole, which is shorter than its diff:
```python
import functools

import jax
import jax.numpy as jnp
from jax import lax
from jax.experimental import pallas as pl
from jax.experimental.pallas import tpu as pltpu
from jax.sharding import PartitionSpec as P

MESH = pl.DeviceIdType.MESH
OCN = 4
CAP = 2
NBR = 4
G = 8
LANES = 128
ORDER = (0, 3, 1, 2)
RIGHT_LAST = (0, 1)
LEFT_LAST = (3, 2)


def distinct(src_ref, low):
    found = [jnp.int32(0)] * NBR
    count = jnp.int32(0)
    for b in range(src_ref.shape[0]):
        slot = src_ref[b] - low
        fresh = (slot >= 0) & (slot < 2 * G)
        for k in range(NBR):
            fresh = fresh & ((count <= k) | (found[k] != slot))
        for k in range(NBR):
            found[k] = jnp.where(fresh & (count == k), slot, found[k])
        count = count + fresh.astype(jnp.int32)
    return found


def kernel(regions, field_ref, pick_ref, src_ref, ocn_ref, w_hbm, out_ref,
           row0, row1, row2, row3, row4, row5, row6, row7, halos, pool, tiles, stage, weights, flat, meta, asked, meta_s, asked_s, place_s, diff, part,
           ring_send, ring_recv, meta_send, meta_recv, halo_send, halo_recv, ask_send, ask_recv,
           nbr_send, nbr_recv, local_sem, w_sem):
    me = lax.axis_index("grp")
    r = lax.axis_index("reg")
    rows = (row0, row1, row2, row3, row4, row5, row6, row7)
    cx = field_ref.shape[1]
    blocks = src_ref.shape[0]
    right, left = lax.rem(me + 1, G), lax.rem(me + G - 1, G)
    has_low, has_high = r > 0, r < regions - 1
    low, high = jnp.maximum(r - 1, 0), jnp.minimum(r + 1, regions - 1)

    def at(offset):
        return lax.rem(me + offset + G, G)

    barrier = pltpu.get_barrier_semaphore()
    for peer in (left, right):
        pl.semaphore_signal(barrier, inc=1, device_id=(peer, r), device_id_type=MESH)

    @pl.when(has_low)
    def _():
        pl.semaphore_signal(barrier, inc=1, device_id=(me, low), device_id_type=MESH)

    @pl.when(has_high)
    def _():
        pl.semaphore_signal(barrier, inc=1, device_id=(me, high), device_id_type=MESH)

    w_copy = pltpu.make_async_copy(w_hbm, weights, w_sem)
    w_copy.start()

    flat[...] = field_ref[...].astype(jnp.float32).reshape(flat.shape)
    for i in range(cx):
        row0[i] = flat[pl.ds(i, row0.shape[1], stride=cx), :].astype(jnp.bfloat16)

    wanted_low, wanted_high = distinct(src_ref, 0), distinct(src_ref, 4 * G)
    lane = lax.broadcasted_iota(jnp.int32, (8, LANES), 1)
    note = jnp.zeros((8, LANES), jnp.int32)
    for k in range(G * CAP):
        note = jnp.where(lane == k, pick_ref[k], note)
    for k in range(NBR):
        note = jnp.where(lane == G * CAP + k, wanted_low[k], note)
        note = jnp.where(lane == G * CAP + NBR + k, wanted_high[k], note)
    meta[me] = note
    for b in range(blocks):
        slot = src_ref[b]
        spot = jnp.int32(2 * G)
        for k in range(1, NBR):
            spot = jnp.where(slot == wanted_low[k], 2 * G + k, spot)
        upper = jnp.int32(2 * G + NBR)
        for k in range(1, NBR):
            upper = jnp.where(slot - 4 * G == wanted_high[k], 2 * G + NBR + k, upper)
        spot = jnp.where(slot >= 2 * G, slot - 2 * G, spot)
        place_s[b] = jnp.where(slot >= 4 * G, upper, spot)

    depth = lax.broadcasted_iota(jnp.int32, (3 * LANES, LANES), 0)
    column = lax.broadcasted_iota(jnp.int32, (3 * LANES, LANES), 1) + LANES
    whole = (jnp.where(depth == column + 1, 0.5, 0.0) - jnp.where(depth == column - 1, 0.5, 0.0)).astype(jnp.float32)
    diff[0] = jnp.where(depth >= LANES, whole, 0.0).astype(jnp.bfloat16)
    diff[1] = whole.astype(jnp.bfloat16)
    diff[2] = jnp.where(depth < 2 * LANES, whole, 0.0).astype(jnp.bfloat16)

    @pl.when(jnp.logical_not(has_low))
    def _():
        for d in range(G):
            halos[0, d] = jnp.zeros(halos.shape[2:], halos.dtype)
        for k in range(NBR):
            tiles[2 * G + k] = jnp.zeros(tiles.shape[1:], tiles.dtype)

    @pl.when(jnp.logical_not(has_high))
    def _():
        for d in range(G):
            halos[1, d] = jnp.zeros(halos.shape[2:], halos.dtype)
        for k in range(NBR):
            tiles[2 * G + NBR + k] = jnp.zeros(tiles.shape[1:], tiles.dtype)

    pl.semaphore_wait(barrier, 2 + has_low.astype(jnp.int32) + has_high.astype(jnp.int32))

    def chunk(offset, c):
        return rows[offset % G].at[pl.ds(2 * c, 2)]

    def ring(way, step, c):
        sign = -1 if way == 0 else 1
        return pltpu.make_async_remote_copy(
            src_ref=chunk(sign * (step - 1), c), dst_ref=chunk(sign * step, c),
            send_sem=ring_send.at[way, step - 1, c], recv_sem=ring_recv.at[way, step - 1, c],
            device_id=(right if way == 0 else left, r), device_id_type=MESH)

    def ring_arrived(way, step, c):
        ring(way, step, c).wait_recv()

    def note_copy(way, step):
        h = at(-(step - 1)) if way == 0 else at(step - 1)
        return pltpu.make_async_remote_copy(
            src_ref=meta.at[h], dst_ref=meta.at[h],
            send_sem=meta_send.at[way, step - 1], recv_sem=meta_recv.at[way, step - 1],
            device_id=(right if way == 0 else left, r), device_id_type=MESH)

    def note_arrived(way, step):
        h = at(-step) if way == 0 else at(step)
        pltpu.make_async_remote_copy(
            src_ref=meta.at[h], dst_ref=meta.at[h],
            send_sem=meta_send.at[way, step - 1], recv_sem=meta_recv.at[way, step - 1],
            device_id=(right if way == 0 else left, r), device_id_type=MESH).wait_recv()

    def to_smem(offset):
        h = at(offset)
        return pltpu.make_async_copy(meta.at[h], meta_s.at[h], local_sem.at[offset % G])

    def halo(way, offset):
        return pltpu.make_async_remote_copy(
            src_ref=rows[offset % G].at[cx - 1 if way == 0 else 0], dst_ref=halos.at[way, offset % G],
            send_sem=halo_send.at[way, offset % G], recv_sem=halo_recv.at[way, offset % G],
            device_id=(me, high if way == 0 else low), device_id_type=MESH)

    def send_halo(way, offset):
        @pl.when(has_high if way == 0 else has_low)
        def _():
            halo(way, offset).start()

    def halos_arrived(offset):
        @pl.when(has_low)
        def _():
            halo(0, offset).wait_recv()

        @pl.when(has_high)
        def _():
            halo(1, offset).wait_recv()

    def ask(way):
        return pltpu.make_async_remote_copy(
            src_ref=meta.at[me], dst_ref=asked.at[way],
            send_sem=ask_send.at[way], recv_sem=ask_recv.at[way],
            device_id=(me, high if way == 0 else low), device_id_type=MESH)

    def neighbour_tile(way, k):
        return pltpu.make_async_remote_copy(
            src_ref=stage.at[way * NBR + k], dst_ref=tiles.at[2 * G + way * NBR + k],
            send_sem=nbr_send.at[way, k], recv_sem=nbr_recv.at[way, k],
            device_id=(me, high if way == 0 else low), device_id_type=MESH)

    for way in range(2):
        note_copy(way, 1).start()
    for c in ORDER:
        for way in range(2):
            ring(way, 1, c).start()
    to_smem(0).start()

    @pl.when(has_high)
    def _():
        ask(0).start()

    @pl.when(has_low)
    def _():
        ask(1).start()

    for way in range(2):
        send_halo(way, 0)

    def make_tiles(offset):
        halos_arrived(offset)
        to_smem(offset).wait()
        h = at(offset)
        here, before, after = rows[offset % G], rows[(offset - 1) % G], rows[(offset + 1) % G]
        kind = jnp.where(h == 0, 0, jnp.where(h == G - 1, 2, 1))
        for c in range(CAP):
            i = meta_s[h, 0, CAP * me + c]
            own = here[i]
            up = jnp.where(i == 0, halos[0, offset % G], here[jnp.maximum(i - 1, 0)]).astype(jnp.float32)
            down = jnp.where(i == cx - 1, halos[1, offset % G], here[jnp.minimum(i + 1, cx - 1)]).astype(jnp.float32)
            grad_x = ((down - up) * 0.5).astype(jnp.bfloat16)
            side = jnp.concatenate([before[i], own, after[i]], axis=1)
            grad_y = jnp.dot(side, diff[kind], preferred_element_type=jnp.float32).astype(jnp.bfloat16)
            whole = jnp.concatenate([own, grad_x, grad_y], axis=1)
            pool[CAP * h + c] = whole
            tiles[CAP * h + c] = whole

    for step in range(1, 5):
        both = step < 4
        note_arrived(0, step)
        if step < 4:
            note_copy(0, step + 1).start()
        to_smem(-step).start()
        if both:
            note_arrived(1, step)
            if step < 3:
                note_copy(1, step + 1).start()
            to_smem(step).start()
        right_order = ORDER if both else RIGHT_LAST
        left_order = ORDER if both else LEFT_LAST
        for c, d in zip(right_order, left_order):
            ring_arrived(0, step, c)
            if step < 3 or (step == 3 and c in RIGHT_LAST):
                ring(0, step + 1, c).start()
            if c == 0:
                send_halo(1, -step)
            if c == 3:
                send_halo(0, -step)
            ring_arrived(1, step, d)
            if step < 3 or (step == 3 and d in LEFT_LAST):
                ring(1, step + 1, d).start()
            if d == 0:
                send_halo(1, step)
            if d == 3:
                send_halo(0, step)
        if step == 1:
            make_tiles(0)
        else:
            make_tiles(-(step - 1))
            make_tiles(step - 1)
    make_tiles(4)

    def serve(way):
        arrived = ask(1 - way)
        arrived.wait_recv()
        to_scalar = pltpu.make_async_copy(asked.at[1 - way], asked_s.at[1 - way], local_sem.at[G + way])
        to_scalar.start()
        to_scalar.wait()
        for k in range(NBR):
            slot = asked_s[1 - way, 0, G * CAP + way * NBR + k]
            stage[way * NBR + k] = pool[slot]
            neighbour_tile(way, k).start()

    @pl.when(has_high)
    def _():
        serve(0)

    @pl.when(has_low)
    def _():
        serve(1)

    w_copy.wait()

    @pl.when(has_low)
    def _():
        for k in range(NBR):
            neighbour_tile(0, k).wait_recv()

    @pl.when(has_high)
    def _():
        for k in range(NBR):
            neighbour_tile(1, k).wait_recv()

    @pl.loop(0, blocks // 4)
    def _(quarter):
        for k in range(4):
            b = quarter * 4 + k
            part[b] = jnp.dot(tiles[place_s[b]], weights[b], preferred_element_type=jnp.float32)

    height = 16

    @pl.loop(0, part.shape[1] // height)
    def _(band):
        here = pl.ds(pl.multiple_of(band * height, height), height)
        sums = [jnp.zeros((height, LANES), jnp.float32) for _ in range(OCN)]
        for b in range(blocks):
            value = part[b, here, :]
            for t in range(OCN):
                sums[t] = sums[t] + value * (ocn_ref[b] == t).astype(jnp.float32)
        for t in range(OCN):
            out_ref[here, t * LANES:(t + 1) * LANES] = sums[t].astype(jnp.bfloat16)

    for step in range(1, 5):
        note_copy(0, step).wait_send()
        if step < 4:
            note_copy(1, step).wait_send()
        for c in ORDER if step < 4 else RIGHT_LAST:
            ring(0, step, c).wait_send()
        for c in ORDER if step < 4 else LEFT_LAST:
            ring(1, step, c).wait_send()

    for way, there in ((0, has_high), (1, has_low)):
        @pl.when(there)
        def _(way=way):
            ask(way).wait_send()
            for offset in range(G):
                halo(way, offset).wait_send()
            for k in range(NBR):
                neighbour_tile(way, k).wait_send()


def solution(mesh):
    regions = mesh.shape["reg"]

    def per_device(field, send_pick, blk_src, blk_ocn, blk_weight):
        channels, cx, cells = field.shape
        blocks = blk_src.shape[0]
        vmem = pl.BlockSpec(memory_space=pltpu.VMEM)
        smem = pl.BlockSpec(memory_space=pltpu.SMEM)
        dma = pltpu.SemaphoreType.DMA
        bf16, f32, i32 = jnp.bfloat16, jnp.float32, jnp.int32
        return pl.pallas_call(
            functools.partial(kernel, regions),
            out_shape=jax.ShapeDtypeStruct((channels, OCN * cells), bf16),
            in_specs=[vmem, smem, smem, smem, pl.BlockSpec(memory_space=pltpu.HBM)],
            out_specs=vmem,
            scratch_shapes=[
                *[pltpu.VMEM((cx, channels, cells), bf16) for _ in range(G)],
                pltpu.VMEM((2, G, channels, cells), bf16),
                pltpu.VMEM((G * CAP, channels, 3 * cells), bf16),
                pltpu.VMEM((G * CAP + 2 * NBR, channels, 3 * cells), bf16),
                pltpu.VMEM((2 * NBR, channels, 3 * cells), bf16),
                pltpu.VMEM((blocks, 3 * cells, cells), bf16),
                pltpu.VMEM((channels * cx, cells), f32),
                pltpu.VMEM((G, 8, LANES), i32),
                pltpu.VMEM((2, 8, LANES), i32),
                pltpu.SMEM((G, 8, LANES), i32),
                pltpu.SMEM((2, 8, LANES), i32),
                pltpu.SMEM((blocks,), i32),
                pltpu.VMEM((3, 3 * cells, cells), bf16),
                pltpu.VMEM((blocks, channels, cells), f32),
                dma((2, 4, 4)), dma((2, 4, 4)),
                dma((2, 4)), dma((2, 4)),
                dma((2, G)), dma((2, G)),
                dma((2,)), dma((2,)),
                dma((2, NBR)), dma((2, NBR)),
                dma((G + 2,)),
                dma,
            ],
            compiler_params=pltpu.CompilerParams(
                collective_id=0, has_side_effects=True, vmem_limit_bytes=40 * 1024 * 1024
            ),
            cost_estimate=pl.CostEstimate(
                flops=2 * blocks * channels * 3 * cells * cells, bytes_accessed=4 * 1024 * 1024, transcendentals=0
            ),
        )(field, send_pick, blk_src, blk_ocn, blk_weight)

    placed = (
        P(None, "reg", "grp"),
        P(("grp", "reg")),
        P(("grp", "reg")),
        P(("grp", "reg")),
        P(("grp", "reg"), None, None),
    )
    return jax.shard_map(
        per_device, mesh=mesh, in_specs=placed, out_specs=P(None, ("grp", "reg")), check_vma=False
    )
```

time: 125 us -> 53.8 us (0.43)
  the two profiles are of different devices: /device:TPU:399 before, /device:TPU:1 now
where the time goes in v1:
time: 53.8 us; the launch traced here: 53.6 us
  Pallas kernels  48.1 us (89%)
  local copies, waits for them, and re-layouts  5.46 us (10%)
    pallas_call x1, Pallas kernels, per_device(): pl.pallas_call(functools.partial(kernel, regions), out_shape=jax.ShapeDty...  48.1 us
    unnamed x11, local copies, waits for them, and re-layouts  5.46 us

profile of v1, /device:TPU:1, one launch (start us, length us, event | category | flops | bytes accessed | tf_op | source)
XLA Modules:
  0.0 53.6 jit_solution(4765756016955039442)
XLA Ops:
  0.0 0.0 copy-start
  0.0 1.9 %copy-done = bf16[32,384,128]{2,1,0:T(8,128)(2,1)S(1)} copy-done((bf16[32,384,128]{2,1,0:T(8,128)(2,1)S(1)}, bf16[32,384,128]{2,1,0:T(8,128)(2,1)}, u32[]{:S(2)}) %copy-start) | copy-done | bytes 3145752
  1.9 0.0 copy-start.1
  1.9 0.9 %copy-done.1 = bf16[128,8,128]{2,1,0:T(8,128)(2,1)S(1)} copy-done((bf16[128,8,128]{2,1,0:T(8,128)(2,1)S(1)}, bf16[128,8,128]{2,1,0:T(8,128)(2,1)}, u32[]{:S(2)}) %copy-start.1) | copy-done | bytes 262168
  2.8 0.0 copy-start.2
  2.8 0.7 %copy-done.2 = s32[16]{0:T(128)S(1)} copy-done((s32[16]{0:T(128)S(1)}, s32[16]{0:T(128)}, u32[]{:S(2)}) %copy-start.2) | copy-done | bytes 88
  3.5 0.0 copy-start.3
  3.5 0.7 %copy-done.3 = s32[32]{0:T(128)S(1)} copy-done((s32[32]{0:T(128)S(1)}, s32[32]{0:T(128)}, u32[]{:S(2)}) %copy-start.3) | copy-done | bytes 152
  4.2 0.0 copy-start.4
  4.2 0.7 %copy-done.4 = s32[32]{0:T(128)S(1)} copy-done((s32[32]{0:T(128)S(1)}, s32[32]{0:T(128)}, u32[]{:S(2)}) %copy-start.4) | copy-done | bytes 152
  4.8 48.1 %shard_map.55 = bf16[128,512]{1,0:T(8,128)(2,1)S(1)} custom-call(bf16[128,8,128]{2,1,0:T(8,128)(2,1)S(1)} %copy-done.1, s32[16]{0:T(128)S(1)} %copy-done.2, s32[32]{0:T(128)S(1)} %copy-done.3, s32[32]{0:T(128)S(1)} %copy-done.4, bf16[32,384,128]{2,1,0:T(8,128)(2,1)S(1)} %copy-done), custom_call_target="tpu_custom_call" | custom-call | flops 402653184 | bytes 4194304 | tf_op jit(solution)/shard_map/pallas_call | solution.py:326
  53.0 0.7 %copy.7 = bf16[128,512]{1,0:T(8,128)(2,1)} copy(bf16[128,512]{1,0:T(8,128)(2,1)S(1)} %shard_map.55) | data formatting | bytes 262144
Async XLA Ops:
  0.0 1.9 %copy-start = (bf16[32,384,128]{2,1,0:T(8,128)(2,1)S(1)}, bf16[32,384,128]{2,1,0:T(8,128)(2,1)}, u32[]{:S(2)}) copy-start(bf16[32,384,128]{2,1,0:T(8,128)(2,1)} %w_hbm.1) | copy-start | bytes 9437188
  1.9 0.9 %copy-start.1 = (bf16[128,8,128]{2,1,0:T(8,128)(2,1)S(1)}, bf16[128,8,128]{2,1,0:T(8,128)(2,1)}, u32[]{:S(2)}) copy-start(bf16[128,8,128]{2,1,0:T(8,128)(2,1)} %field_ref.1) | copy-start | bytes 786436
  2.8 0.7 %copy-start.2 = (s32[16]{0:T(128)S(1)}, s32[16]{0:T(128)}, u32[]{:S(2)}) copy-start(s32[16]{0:T(128)} %pick_ref.1) | copy-start | bytes 196
  3.5 0.7 %copy-start.3 = (s32[32]{0:T(128)S(1)}, s32[32]{0:T(128)}, u32[]{:S(2)}) copy-start(s32[32]{0:T(128)} %src_ref.1) | copy-start | bytes 388
  4.2 0.7 %copy-start.4 = (s32[32]{0:T(128)S(1)}, s32[32]{0:T(128)}, u32[]{:S(2)}) copy-start(s32[32]{0:T(128)} %ocn_ref.1) | copy-start | bytes 388

commit v2 on v0

v2 whole, which is shorter than its diff:
```python
import functools

import jax
import jax.numpy as jnp
from jax import lax
from jax.experimental import pallas as pl
from jax.experimental.pallas import tpu as pltpu
from jax.sharding import PartitionSpec as P

MESH = pl.DeviceIdType.MESH
OCN = 4
CAP = 2
NBR = 4
G = 8
LANES = 128
VMEM_LIMIT = 48 * 1024 * 1024
ORDER = (0, 3, 1, 2)
OWN = G * CAP
EARLY, LATE = OWN, OWN + 2 * NBR
SLOTS = LATE + 2 * CAP


def transposed(matrix, unit):
    return lax.dot_general(
        unit, matrix, (((1,), (1,)), ((), ())), preferred_element_type=jnp.float32
    ).astype(jnp.bfloat16)


def distinct(src_ref, low):
    found = [jnp.int32(0)] * NBR
    count = jnp.int32(0)
    for b in range(src_ref.shape[0]):
        slot = src_ref[b] - low
        fresh = (slot >= 0) & (slot < OWN)
        for k in range(NBR):
            fresh = fresh & ((count <= k) | (found[k] != slot))
        for k in range(NBR):
            found[k] = jnp.where(fresh & (count == k), slot, found[k])
        count = count + fresh.astype(jnp.int32)
    return found


def kernel(regions, field_hbm, pick_hbm, src_hbm, ocn_hbm, w_hbm, out_ref,
           field_ref, pick_ref, src_ref, ocn_ref,
           row0, row1, row2, row3, row5, row6, row7, halos, edges, wish, fringe,
           pass3, pass4, got3, got4, pool, tiles, stage, near, late, weights, flat,
           meta, asked, meta_s, asked_s, place_s, band, part, fringe_out,
           ring_send, ring_recv, pass_send, pass_recv, meta_send, meta_recv, edge_send, edge_recv,
           halo_send, halo_recv, ask_send, ask_recv, near_send, near_recv, fringe_send, fringe_recv,
           late_send, late_recv, local_sem, in_sem, w_sem):
    me = lax.axis_index("grp")
    r = lax.axis_index("reg")
    rows = {0: row0, 1: row1, 2: row2, 3: row3, -3: row5, -2: row6, -1: row7}
    channels, cx = field_ref.shape[:2]
    half = channels // 2
    first, second = pl.ds(0, half), pl.ds(half, half)
    raw_half = (first, second)
    blocks = src_ref.shape[0]
    f32, bf16 = jnp.float32, jnp.bfloat16
    right, left = lax.rem(me + 1, G), lax.rem(me + G - 1, G)
    has_low, has_high = r > 0, r < regions - 1
    low, high = jnp.maximum(r - 1, 0), jnp.minimum(r + 1, regions - 1)
    there = (has_high, has_low)

    def at(offset):
        return lax.rem(me + offset + G, G)

    def along(way):
        return (right if way == 0 else left, r)

    def across(way):
        return (me, high if way == 0 else low)

    def remote(source, target, send, receive, device):
        return pltpu.make_async_remote_copy(
            src_ref=source, dst_ref=target, send_sem=send, recv_sem=receive, device_id=device, device_id_type=MESH)

    arriving = [
        pltpu.make_async_copy(origin, here, in_sem.at[k])
        for k, (origin, here) in enumerate(
            ((field_hbm, field_ref), (pick_hbm, pick_ref), (src_hbm, src_ref), (ocn_hbm, ocn_ref)))
    ]
    for copy in arriving:
        copy.start()
    barrier = pltpu.get_barrier_semaphore()
    for way in range(2):
        pl.semaphore_signal(barrier, inc=1, device_id=along(way), device_id_type=MESH)

    for way in range(2):
        @pl.when(there[way])
        def _(way=way):
            pl.semaphore_signal(barrier, inc=1, device_id=across(way), device_id_type=MESH)

    w_copy = pltpu.make_async_copy(w_hbm, weights, w_sem)
    w_copy.start()

    fringe[...] = jnp.zeros(fringe.shape, bf16)
    for c in range(CAP):
        pool[CAP * at(4) + c] = jnp.zeros(pool.shape[1:], bf16)

    for way in range(2):
        @pl.when(jnp.logical_not(there[1 - way]))
        def _(way=way):
            for d in range(G):
                halos[way, d] = jnp.zeros(halos.shape[2:], bf16)
            for k in range(NBR):
                tiles[EARLY + way * NBR + k] = jnp.zeros(tiles.shape[1:], bf16)
            for c in range(CAP):
                tiles[LATE + way * CAP + c] = jnp.zeros(tiles.shape[1:], bf16)

    arriving[0].wait()
    flat[...] = field_ref[...].astype(f32).reshape(flat.shape)
    for i in range(cx):
        row0[i] = flat[pl.ds(i, channels, stride=cx), :].astype(bf16)

    pl.semaphore_wait(barrier, 2 + has_low.astype(jnp.int32) + has_high.astype(jnp.int32))

    def ring(way, step, c):
        sign = -1 if way == 0 else 1
        source = rows[sign * (step - 1)].at[pl.ds(2 * c, 2)]
        if step == 3:
            source = rows[sign * 2].at[pl.ds(2 * c, 2), raw_half[way]]
        return remote(source, rows[sign * step].at[pl.ds(2 * c, 2)],
                      ring_send.at[way, step - 1, c], ring_recv.at[way, step - 1, c], along(way))

    def passed(way, step):
        source, target = (pass3, got3) if step == 3 else (pass4, got4)
        return remote(source.at[way], target.at[way],
                      pass_send.at[way, step - 3], pass_recv.at[way, step - 3], along(way))

    def note_copy(way, step, receiving=False):
        sign = -1 if way == 0 else 1
        h = at(sign * (step if receiving else step - 1))
        return remote(meta.at[h], meta.at[h], meta_send.at[way, step - 1], meta_recv.at[way, step - 1], along(way))

    def edge_copy(way, step, receiving=False):
        sign = -1 if way == 0 else 1
        h = at(sign * (step if receiving else step - 1))
        return remote(edges.at[h], edges.at[h], edge_send.at[way, step - 1], edge_recv.at[way, step - 1], along(way))

    def to_smem(offset):
        h = at(offset)
        return pltpu.make_async_copy(meta.at[h], meta_s.at[h], local_sem.at[offset % G])

    def halo(way, offset):
        source = rows[offset].at[cx - 1 if way == 0 else 0]
        target = halos.at[way, offset % G]
        if abs(offset) == 3:
            target = halos.at[way, offset % G, first if offset < 0 else second]
        return remote(source, target, halo_send.at[way, offset % G], halo_recv.at[way, offset % G], across(way))

    def send_halo(way, offset):
        @pl.when(there[way])
        def _():
            halo(way, offset).start()

    def halos_arrived(offset):
        for way in range(2):
            @pl.when(there[1 - way])
            def _(way=way):
                halo(way, offset).wait_recv()

    def ask(way):
        return remote(wish, asked.at[way], ask_send.at[way], ask_recv.at[way], across(way))

    def near_copy(way, k):
        return remote(stage.at[way, k], near.at[way, k], near_send.at[way, k], near_recv.at[way, k], across(way))

    def fringe_copy(way):
        return remote(fringe_out.at[way], fringe.at[pl.ds(16 * way, 16)],
                      fringe_send.at[way], fringe_recv.at[way], across(way))

    def late_copy(way, chain):
        return remote(got4.at[chain], late.at[way, chain],
                      late_send.at[way, chain], late_recv.at[way, chain], across(way))

    for c in ORDER:
        for way in range(2):
            ring(way, 1, c).start()
        if c == 3:
            for way in range(2):
                send_halo(way, 0)

    for copy in arriving[1:]:
        copy.wait()
    lane = lax.broadcasted_iota(jnp.int32, (8, LANES), 1)
    note = jnp.zeros((8, LANES), jnp.int32)
    for k in range(OWN):
        note = jnp.where(lane == k, pick_ref[k], note)
    meta[me] = note
    line = lax.broadcasted_iota(jnp.int32, (16, LANES), 0)
    spot = lax.broadcasted_iota(jnp.int32, (16, LANES), 1)
    border = jnp.zeros((16, channels), f32)
    for i in range(cx):
        chosen = ((line == i) & (spot == 0)) | ((line == 8 + i) & (spot == LANES - 1))
        border = border + lax.dot_general(
            jnp.where(chosen, 1.0, 0.0).astype(bf16), row0[i], (((1,), (1,)), ((), ())), preferred_element_type=f32)
    edges[me] = border.astype(bf16)
    for way in range(2):
        note_copy(way, 1).start()
        edge_copy(way, 1).start()
    to_smem(0).start()

    wanted = (distinct(src_ref, 0), distinct(src_ref, 2 * OWN))
    request = jnp.zeros((8, LANES), jnp.int32)
    for way in range(2):
        for k in range(NBR):
            request = jnp.where(lane == way * NBR + k, wanted[way][k], request)
    wish[...] = request
    for way in range(2):
        @pl.when(there[way])
        def _(way=way):
            ask(way).start()
    far = CAP * at(4)
    for b in range(blocks):
        slot = src_ref[b]
        found = []
        for way in range(2):
            named = slot - 2 * OWN * way
            where = jnp.int32(EARLY + way * NBR)
            for k in range(1, NBR):
                where = jnp.where(named == wanted[way][k], EARLY + way * NBR + k, where)
            for c in range(CAP):
                where = jnp.where(named == far + c, LATE + way * CAP + c, where)
            found.append(where)
        place_s[b] = jnp.where(slot < OWN, found[0], jnp.where(slot < 2 * OWN, slot - OWN, found[1]))

    depth = lax.broadcasted_iota(jnp.int32, (LANES, LANES), 0)
    column = lax.broadcasted_iota(jnp.int32, (LANES, LANES), 1)
    band[0] = (jnp.where(depth == column + 1, 0.5, 0.0) - jnp.where(depth == column - 1, 0.5, 0.0)).astype(bf16)
    band[1] = jnp.where(depth == column, 1.0, 0.0).astype(bf16)

    def picked(h, group, c):
        return meta_s[h, 0, CAP * group + c]

    def raw_pair(offset, i, span):
        tile = rows[offset]
        own_span = pl.ds(0, half) if abs(offset) == 3 else span
        own = tile[i, own_span, :]
        up = jnp.where(i == 0, halos[0, offset % G, span, :], tile[jnp.maximum(i - 1, 0), own_span, :]).astype(f32)
        down = jnp.where(
            i == cx - 1, halos[1, offset % G, span, :], tile[jnp.minimum(i + 1, cx - 1), own_span, :]).astype(f32)
        return own, ((down - up) * 0.5).astype(bf16)

    def pass_on(step):
        for way in range(2):
            offset = -(step - 1) if way == 0 else step - 1
            span = raw_half[1 - way] if step == 3 else raw_half[way]
            target = pass3 if step == 3 else pass4
            for c in range(CAP):
                i = picked(at(offset), along(way)[0], c)
                own, grad_x = raw_pair(offset, i, span)
                target[way, c, 0] = own
                target[way, c, 1] = grad_x
            passed(way, step).start()

    def with_border(own, corners, prior, following):
        ends = (jnp.where((depth == following) & (column == LANES - 1), 0.5, 0.0)
                - jnp.where((depth == prior) & (column == 0), 0.5, 0.0)).astype(bf16)
        return jnp.dot(
            jnp.concatenate([own, corners], axis=1), jnp.concatenate([band[0], ends], axis=0),
            preferred_element_type=f32).astype(bf16)

    def keep(offset, pairs, corners):
        h = at(offset)
        for c in range(CAP):
            i = picked(h, me, c)
            own, grad_x = pairs(c, i)
            grad_y = with_border(own, corners, 16 * (h - 1) + 8 + i, 16 * (h + 1) + i)
            whole = jnp.concatenate([own, grad_x, grad_y], axis=1)
            pool[CAP * h + c] = whole
            tiles[CAP * h + c] = whole

    for step in range(1, 5):
        ways = (0, 1) if step < 4 else (0,)
        for way in ways:
            note_copy(way, step, True).wait_recv()
            edge_copy(way, step, True).wait_recv()
            if step < 3 or (step == 3 and way == 0):
                note_copy(way, step + 1).start()
                edge_copy(way, step + 1).start()
            to_smem(-step if way == 0 else step).start()
        if step == 4:
            break
        for c in ORDER:
            for way in range(2):
                ring(way, step, c).wait_recv()
                if step < 3:
                    ring(way, step + 1, c).start()
                offset = -step if way == 0 else step
                if c == 0:
                    send_halo(1, offset)
                if c == 3:
                    send_halo(0, offset)
        if step >= 2:
            for offset in (-step, step):
                halos_arrived(offset)
                to_smem(offset).wait()
            pass_on(step + 1)

    for offset in (0, -1, 1):
        halos_arrived(offset)
        to_smem(offset).wait()
    to_smem(-4).wait()
    everything = pl.ds(0, channels)
    corners = transposed(edges[...].reshape(G * 16, channels), band[1])
    for offset in (0, -1, 1, -2, 2):
        keep(offset, lambda c, i, offset=offset: raw_pair(offset, i, everything), corners)
    for way, offset in ((0, -3), (1, 3)):
        passed(way, 3).wait_recv()

        def pairs(c, i, way=way, offset=offset):
            raw = raw_pair(offset, i, raw_half[way])
            come = (got3[way, c, 0], got3[way, c, 1])
            return tuple(
                jnp.concatenate([a, b] if way == 0 else [b, a], axis=0) for a, b in zip(raw, come))

        keep(offset, pairs, corners)

    def serve(way):
        ask(1 - way).wait_recv()
        to_scalar = pltpu.make_async_copy(asked.at[1 - way], asked_s.at[1 - way], local_sem.at[G + way])
        to_scalar.start()
        to_scalar.wait()
        chosen = jnp.zeros((16, G * 16), f32)
        slots = [asked_s[1 - way, 0, way * NBR + k] for k in range(NBR)] + [far + c for c in range(CAP)]
        for k, slot in enumerate(slots):
            if k < NBR:
                stage[way, k, 0] = pool[slot, :, :LANES]
                stage[way, k, 1] = pool[slot, :, LANES:2 * LANES]
                near_copy(way, k).start()
            h = lax.shift_right_logical(slot, 1)
            i = picked(h, me, slot - 2 * h)
            chosen = jnp.where((line == 2 * k) & (spot == 16 * (h - 1) + 8 + i), 1.0, chosen)
            chosen = jnp.where((line == 2 * k + 1) & (spot == 16 * (h + 1) + i), 1.0, chosen)
        fringe_out[way] = jnp.dot(
            chosen.astype(bf16), edges[...].reshape(G * 16, channels), preferred_element_type=f32).astype(bf16)
        fringe_copy(way).start()

    for way in range(2):
        @pl.when(there[way])
        def _(way=way):
            serve(way)

    for chain in range(2):
        passed(chain, 4).wait_recv()
        for way in range(2):
            @pl.when(there[way])
            def _(way=way):
                late_copy(way, chain).start()
    keep(4, lambda c, i: tuple(jnp.concatenate([got4[0, c, p], got4[1, c, p]], axis=0) for p in range(2)), corners)

    def from_neighbour(way, k, own, grad_x, sides):
        grad_y = with_border(own, sides, 16 * way + 2 * k, 16 * way + 2 * k + 1)
        return jnp.concatenate([own, grad_x, grad_y], axis=1)

    for way in range(2):
        @pl.when(there[1 - way])
        def _(way=way):
            fringe_copy(way).wait_recv()
            for k in range(NBR):
                near_copy(way, k).wait_recv()
    sides = transposed(fringe[...], band[1])
    for way in range(2):
        @pl.when(there[1 - way])
        def _(way=way):
            for k in range(NBR):
                tiles[EARLY + way * NBR + k] = from_neighbour(way, k, near[way, k, 0], near[way, k, 1], sides)
    w_copy.wait()
    for way in range(2):
        @pl.when(there[1 - way])
        def _(way=way):
            for chain in range(2):
                late_copy(way, chain).wait_recv()
            for c in range(CAP):
                own, grad_x = (
                    jnp.concatenate([late[way, 0, c, p], late[way, 1, c, p]], axis=0) for p in range(2))
                tiles[LATE + way * CAP + c] = from_neighbour(way, NBR + c, own, grad_x, sides)

    @pl.loop(0, blocks // 4)
    def _(quarter):
        for k in range(4):
            b = quarter * 4 + k
            part[b] = jnp.dot(tiles[place_s[b]], weights[b], preferred_element_type=f32)

    height = 16

    @pl.loop(0, channels // height)
    def _(strip):
        here = pl.ds(pl.multiple_of(strip * height, height), height)
        sums = [jnp.zeros((height, LANES), f32) for _ in range(OCN)]
        for b in range(blocks):
            value = part[b, here, :]
            for t in range(OCN):
                sums[t] = sums[t] + value * (ocn_ref[b] == t).astype(f32)
        for t in range(OCN):
            out_ref[here, t * LANES:(t + 1) * LANES] = sums[t].astype(bf16)

    for way in range(2):
        for step in range(1, 4):
            for c in ORDER:
                ring(way, step, c).wait_send()
        for step in (3, 4):
            passed(way, step).wait_send()
        for step in range(1, 5 - way):
            note_copy(way, step).wait_send()
            edge_copy(way, step).wait_send()

        @pl.when(there[way])
        def _(way=way):
            ask(way).wait_send()
            for offset in rows:
                halo(way, offset).wait_send()
            for k in range(NBR):
                near_copy(way, k).wait_send()
            fringe_copy(way).wait_send()
            for chain in range(2):
                late_copy(way, chain).wait_send()


def solution(mesh):
    regions = mesh.shape["reg"]

    def per_device(field, send_pick, blk_src, blk_ocn, blk_weight):
        channels, cx, cells = field.shape
        blocks = blk_src.shape[0]
        half = channels // 2
        dma = pltpu.SemaphoreType.DMA
        bf16, f32, i32 = jnp.bfloat16, jnp.float32, jnp.int32
        operands = [
            pltpu.with_memory_space_constraint(x, pltpu.HBM) for x in (field, send_pick, blk_src, blk_ocn, blk_weight)
        ]
        return pl.pallas_call(
            functools.partial(kernel, regions),
            out_shape=jax.ShapeDtypeStruct((channels, OCN * cells), bf16),
            in_specs=[pl.BlockSpec(memory_space=pl.ANY)] * 5,
            out_specs=pl.BlockSpec(memory_space=pltpu.VMEM),
            scratch_shapes=[
                pltpu.VMEM(field.shape, bf16),
                pltpu.SMEM(send_pick.shape, i32),
                pltpu.SMEM(blk_src.shape, i32),
                pltpu.SMEM(blk_ocn.shape, i32),
                pltpu.VMEM((cx, channels, cells), bf16),
                pltpu.VMEM((cx, channels, cells), bf16),
                pltpu.VMEM((cx, channels, cells), bf16),
                pltpu.VMEM((cx, half, cells), bf16),
                pltpu.VMEM((cx, half, cells), bf16),
                pltpu.VMEM((cx, channels, cells), bf16),
                pltpu.VMEM((cx, channels, cells), bf16),
                pltpu.VMEM((2, G, channels, cells), bf16),
                pltpu.VMEM((G, 16, channels), bf16),
                pltpu.VMEM((8, LANES), i32),
                pltpu.VMEM((LANES, channels), bf16),
                pltpu.VMEM((2, CAP, 2, half, cells), bf16),
                pltpu.VMEM((2, CAP, 2, half, cells), bf16),
                pltpu.VMEM((2, CAP, 2, half, cells), bf16),
                pltpu.VMEM((2, CAP, 2, half, cells), bf16),
                pltpu.VMEM((OWN, channels, 3 * cells), bf16),
                pltpu.VMEM((SLOTS, channels, 3 * cells), bf16),
                pltpu.VMEM((2, NBR, 2, channels, cells), bf16),
                pltpu.VMEM((2, NBR, 2, channels, cells), bf16),
                pltpu.VMEM((2, 2, CAP, 2, half, cells), bf16),
                pltpu.VMEM((blocks, 3 * cells, cells), bf16),
                pltpu.VMEM((channels * cx, cells), f32),
                pltpu.VMEM((G, 8, LANES), i32),
                pltpu.VMEM((2, 8, LANES), i32),
                pltpu.SMEM((G, 8, LANES), i32),
                pltpu.SMEM((2, 8, LANES), i32),
                pltpu.SMEM((blocks,), i32),
                pltpu.VMEM((2, LANES, LANES), bf16),
                pltpu.VMEM((blocks, channels, cells), f32),
                pltpu.VMEM((2, 16, channels), bf16),
                dma((2, 3, 4)), dma((2, 3, 4)),
                dma((2, 2)), dma((2, 2)),
                dma((2, 4)), dma((2, 4)),
                dma((2, 4)), dma((2, 4)),
                dma((2, G)), dma((2, G)),
                dma((2,)), dma((2,)),
                dma((2, NBR)), dma((2, NBR)),
                dma((2,)), dma((2,)),
                dma((2, 2)), dma((2, 2)),
                dma((G + 2,)),
                dma((4,)),
                dma,
            ],
            compiler_params=pltpu.CompilerParams(
                collective_id=0, has_side_effects=True, vmem_limit_bytes=VMEM_LIMIT
            ),
            cost_estimate=pl.CostEstimate(
                flops=2 * blocks * channels * 3 * cells * cells, bytes_accessed=4 * 1024 * 1024, transcendentals=0
            ),
        )(*operands)

    placed = (
        P(None, "reg", "grp"),
        P(("grp", "reg")),
        P(("grp", "reg")),
        P(("grp", "reg")),
        P(("grp", "reg"), None, None),
    )
    return jax.shard_map(
        per_device, mesh=mesh, in_specs=placed, out_specs=P(None, ("grp", "reg")), check_vma=False
    )
```

time: 125 us -> 49.5 us (0.40)
  the two profiles are of different devices: /device:TPU:399 before, /device:TPU:1 now
where the time goes in v2:
time: 49.5 us; the launch traced here: 49.4 us
  Pallas kernels  48.7 us (98%)
  local copies, waits for them, and re-layouts  0.66 us (1%)
    pallas_call x1, Pallas kernels, per_device(): pl.pallas_call(functools.partial(kernel, regions), out_shape=jax.ShapeDty...  48.7 us

profile of v2, /device:TPU:1, one launch (start us, length us, event | category | flops | bytes accessed | tf_op | source)
XLA Modules:
  0.0 49.4 jit_solution(8706167495772600425)
XLA Ops:
  0.0 48.7 %shard_map.55 = bf16[128,512]{1,0:T(8,128)(2,1)S(1)} custom-call(bf16[128,8,128]{2,1,0:T(8,128)(2,1)} %field_hbm.1, s32[16]{0:T(128)} %pick_hbm.1, s32[32]{0:T(128)} %src_hbm.1, s32[32]{0:T(128)} %ocn_hbm.1, bf16[32,384,128]{2,1,0:T(8,128)(2,1)} %w_hbm.1), custom_call_target="tpu_custom_call" | custom-call | flops 402653184 | bytes 4194304 | tf_op jit(solution)/shard_map/pallas_call | solution.py:433
  48.7 0.7 %copy.7 = bf16[128,512]{1,0:T(8,128)(2,1)} copy(bf16[128,512]{1,0:T(8,128)(2,1)S(1)} %shard_map.55) | data formatting | bytes 262144

commit v3 on v2

--- a/solution.py
+++ b/solution.py
@@ -17,7 +17,8 @@
 ORDER = (0, 3, 1, 2)
 OWN = G * CAP
 EARLY, LATE = OWN, OWN + 2 * NBR
-SLOTS = LATE + 2 * CAP
+LAST = (-3, 3, 4)
+SLOTS = LATE + 2 * CAP * len(LAST)
 
 
 def transposed(matrix, unit):
@@ -43,8 +44,8 @@
 def kernel(regions, field_hbm, pick_hbm, src_hbm, ocn_hbm, w_hbm, out_ref,
            field_ref, pick_ref, src_ref, ocn_ref,
            row0, row1, row2, row3, row5, row6, row7, halos, edges, wish, fringe,
-           pass3, pass4, got3, got4, pool, tiles, stage, near, late, weights, flat,
-           meta, asked, meta_s, asked_s, place_s, band, part, fringe_out,
+           pass3, pass4, got3, got4, raw3, pairs, tiles, stage, near, late, weights, flat,
+           meta, asked, meta_s, asked_s, place_s, band, part_a, part_b, sums, fringe_out,
            ring_send, ring_recv, pass_send, pass_recv, meta_send, meta_recv, edge_send, edge_recv,
            halo_send, halo_recv, ask_send, ask_recv, near_send, near_recv, fringe_send, fringe_recv,
            late_send, late_recv, local_sem, in_sem, w_sem):
@@ -95,8 +96,9 @@
     w_copy.start()
 
     fringe[...] = jnp.zeros(fringe.shape, bf16)
-    for c in range(CAP):
-        pool[CAP * at(4) + c] = jnp.zeros(pool.shape[1:], bf16)
+    for offset in LAST:
+        for c in range(CAP):
+            pairs[CAP * at(offset) + c] = jnp.zeros(pairs.shape[1:], bf16)
 
     for way in range(2):
         @pl.when(jnp.logical_not(there[1 - way]))
@@ -105,8 +107,8 @@
                 halos[way, d] = jnp.zeros(halos.shape[2:], bf16)
             for k in range(NBR):
                 tiles[EARLY + way * NBR + k] = jnp.zeros(tiles.shape[1:], bf16)
-            for c in range(CAP):
-                tiles[LATE + way * CAP + c] = jnp.zeros(tiles.shape[1:], bf16)
+            for k in range(CAP * len(LAST)):
+                tiles[LATE + way * CAP * len(LAST) + k] = jnp.zeros(tiles.shape[1:], bf16)
 
     arriving[0].wait()
     flat[...] = field_ref[...].astype(f32).reshape(flat.shape)
@@ -167,12 +169,18 @@
         return remote(stage.at[way, k], near.at[way, k], near_send.at[way, k], near_recv.at[way, k], across(way))
 
     def fringe_copy(way):
-        return remote(fringe_out.at[way], fringe.at[pl.ds(16 * way, 16)],
+        return remote(fringe_out.at[way], fringe.at[pl.ds(32 * way, 32)],
                       fringe_send.at[way], fringe_recv.at[way], across(way))
 
-    def late_copy(way, chain):
-        return remote(got4.at[chain], late.at[way, chain],
-                      late_send.at[way, chain], late_recv.at[way, chain], across(way))
+    def late_copy(way, kind, chain):
+        return remote((raw3, got3, got4)[kind].at[chain], late.at[way, kind, chain],
+                      late_send.at[way, kind, chain], late_recv.at[way, kind, chain], across(way))
+
+    def send_late(kind, chain):
+        for way in range(2):
+            @pl.when(there[way])
+            def _(way=way):
+                late_copy(way, kind, chain).start()
 
     for c in ORDER:
         for way in range(2):
@@ -211,7 +219,7 @@
         @pl.when(there[way])
         def _(way=way):
             ask(way).start()
-    far = CAP * at(4)
+    far = [CAP * at(offset) + c for offset in LAST for c in range(CAP)]
     for b in range(blocks):
         slot = src_ref[b]
         found = []
@@ -220,8 +228,8 @@
             where = jnp.int32(EARLY + way * NBR)
             for k in range(1, NBR):
                 where = jnp.where(named == wanted[way][k], EARLY + way * NBR + k, where)
-            for c in range(CAP):
-                where = jnp.where(named == far + c, LATE + way * CAP + c, where)
+            for k, slot_of in enumerate(far):
+                where = jnp.where(named == slot_of, LATE + way * len(far) + k, where)
             found.append(where)
         place_s[b] = jnp.where(slot < OWN, found[0], jnp.where(slot < 2 * OWN, slot - OWN, found[1]))
 
@@ -261,16 +269,41 @@
             jnp.concatenate([own, corners], axis=1), jnp.concatenate([band[0], ends], axis=0),
             preferred_element_type=f32).astype(bf16)
 
-    def keep(offset, pairs, corners):
+    def joined(a, b):
+        return jnp.concatenate([a, b], axis=0)
+
+    def keep(offset, pair, corners):
         h = at(offset)
         for c in range(CAP):
             i = picked(h, me, c)
-            own, grad_x = pairs(c, i)
+            own, grad_x = pair(h, c)
             grad_y = with_border(own, corners, 16 * (h - 1) + 8 + i, 16 * (h + 1) + i)
             whole = jnp.concatenate([own, grad_x, grad_y], axis=1)
-            pool[CAP * h + c] = whole
             tiles[CAP * h + c] = whole
 
+    def serve(way):
+        ask(1 - way).wait_recv()
+        to_scalar = pltpu.make_async_copy(asked.at[1 - way], asked_s.at[1 - way], local_sem.at[G + way])
+        to_scalar.start()
+        to_scalar.wait()
+        for k in range(NBR):
+            stage[way, k] = pairs[asked_s[1 - way, 0, way * NBR + k]]
+            near_copy(way, k).start()
+
+    def send_fringe(way):
+        row = lax.broadcasted_iota(jnp.int32, (32, LANES), 0)
+        place = lax.broadcasted_iota(jnp.int32, (32, LANES), 1)
+        chosen = jnp.zeros((32, LANES), f32)
+        for k, slot in enumerate([asked_s[1 - way, 0, way * NBR + k] for k in range(NBR)] + far):
+            h = lax.shift_right_logical(slot, 1)
+            i = picked(h, me, slot - 2 * h)
+            chosen = jnp.where((row == 2 * k) & (place == 16 * (h - 1) + 8 + i), 1.0, chosen)
+            chosen = jnp.where((row == 2 * k + 1) & (place == 16 * (h + 1) + i), 1.0, chosen)
+        fringe_out[way] = jnp.dot(
+            chosen.astype(bf16), edges[...].reshape(G * 16, channels), preferred_element_type=f32).astype(bf16)
+        fringe_copy(way).start()
+
+    everything = pl.ds(0, channels)
     for step in range(1, 5):
         ways = (0, 1) if step < 4 else (0,)
         for way in ways:
@@ -297,61 +330,48 @@
                 halos_arrived(offset)
                 to_smem(offset).wait()
             pass_on(step + 1)
-
-    for offset in (0, -1, 1):
-        halos_arrived(offset)
-        to_smem(offset).wait()
+        if step == 2:
+            for offset in (0, -1, 1):
+                halos_arrived(offset)
+                to_smem(offset).wait()
+            for offset in (0, -1, 1, -2, 2):
+                for c in range(CAP):
+                    h = at(offset)
+                    own, grad_x = raw_pair(offset, picked(h, me, c), everything)
+                    pairs[CAP * h + c, 0] = own
+                    pairs[CAP * h + c, 1] = grad_x
+            for way in range(2):
+                @pl.when(there[way])
+                def _(way=way):
+                    serve(way)
+        if step == 3:
+            for way, offset in ((0, -3), (1, 3)):
+                for c in range(CAP):
+                    own, grad_x = raw_pair(offset, picked(at(offset), me, c), raw_half[way])
+                    raw3[way, c, 0] = own
+                    raw3[way, c, 1] = grad_x
+                send_late(0, way)
+
     to_smem(-4).wait()
-    everything = pl.ds(0, channels)
+    for chain in range(2):
+        passed(chain, 3).wait_recv()
+        send_late(1, chain)
+    for way in range(2):
+        @pl.when(there[way])
+        def _(way=way):
+            send_fringe(way)
     corners = transposed(edges[...].reshape(G * 16, channels), band[1])
     for offset in (0, -1, 1, -2, 2):
-        keep(offset, lambda c, i, offset=offset: raw_pair(offset, i, everything), corners)
-    for way, offset in ((0, -3), (1, 3)):
-        passed(way, 3).wait_recv()
-
-        def pairs(c, i, way=way, offset=offset):
-            raw = raw_pair(offset, i, raw_half[way])
-            come = (got3[way, c, 0], got3[way, c, 1])
-            return tuple(
-                jnp.concatenate([a, b] if way == 0 else [b, a], axis=0) for a, b in zip(raw, come))
-
-        keep(offset, pairs, corners)
-
-    def serve(way):
-        ask(1 - way).wait_recv()
-        to_scalar = pltpu.make_async_copy(asked.at[1 - way], asked_s.at[1 - way], local_sem.at[G + way])
-        to_scalar.start()
-        to_scalar.wait()
-        chosen = jnp.zeros((16, G * 16), f32)
-        slots = [asked_s[1 - way, 0, way * NBR + k] for k in range(NBR)] + [far + c for c in range(CAP)]
-        for k, slot in enumerate(slots):
-            if k < NBR:
-                stage[way, k, 0] = pool[slot, :, :LANES]
-                stage[way, k, 1] = pool[slot, :, LANES:2 * LANES]
-                near_copy(way, k).start()
-            h = lax.shift_right_logical(slot, 1)
-            i = picked(h, me, slot - 2 * h)
-            chosen = jnp.where((line == 2 * k) & (spot == 16 * (h - 1) + 8 + i), 1.0, chosen)
-            chosen = jnp.where((line == 2 * k + 1) & (spot == 16 * (h + 1) + i), 1.0, chosen)
-        fringe_out[way] = jnp.dot(
-            chosen.astype(bf16), edges[...].reshape(G * 16, channels), preferred_element_type=f32).astype(bf16)
-        fringe_copy(way).start()
-
-    for way in range(2):
-        @pl.when(there[way])
-        def _(way=way):
-            serve(way)
-
+        keep(offset, lambda h, c: (pairs[CAP * h + c, 0], pairs[CAP * h + c, 1]), corners)
+    keep(-3, lambda h, c: tuple(joined(raw3[0, c, p], got3[0, c, p]) for p in range(2)), corners)
+    keep(3, lambda h, c: tuple(joined(got3[1, c, p], raw3[1, c, p]) for p in range(2)), corners)
     for chain in range(2):
         passed(chain, 4).wait_recv()
-        for way in range(2):
-            @pl.when(there[way])
-            def _(way=way):
-                late_copy(way, chain).start()
-    keep(4, lambda c, i: tuple(jnp.concatenate([got4[0, c, p], got4[1, c, p]], axis=0) for p in range(2)), corners)
+        send_late(2, chain)
+    keep(4, lambda h, c: tuple(joined(got4[0, c, p], got4[1, c, p]) for p in range(2)), corners)
 
     def from_neighbour(way, k, own, grad_x, sides):
-        grad_y = with_border(own, sides, 16 * way + 2 * k, 16 * way + 2 * k + 1)
+        grad_y = with_border(own, sides, 32 * way + 2 * k, 32 * way + 2 * k + 1)
         return jnp.concatenate([own, grad_x, grad_y], axis=1)
 
     for way in range(2):
@@ -367,34 +387,53 @@
             for k in range(NBR):
                 tiles[EARLY + way * NBR + k] = from_neighbour(way, k, near[way, k, 0], near[way, k, 1], sides)
     w_copy.wait()
-    for way in range(2):
-        @pl.when(there[1 - way])
-        def _(way=way):
-            for chain in range(2):
-                late_copy(way, chain).wait_recv()
-            for c in range(CAP):
-                own, grad_x = (
-                    jnp.concatenate([late[way, 0, c, p], late[way, 1, c, p]], axis=0) for p in range(2))
-                tiles[LATE + way * CAP + c] = from_neighbour(way, NBR + c, own, grad_x, sides)
-
-    @pl.loop(0, blocks // 4)
-    def _(quarter):
+
+    def late_tile(way, offset, c):
+        halves = {-3: ((0, 0), (1, 0)), 3: ((1, 1), (0, 1)), 4: ((2, 0), (2, 1))}[offset]
+        own, grad_x = (joined(*[late[way, kind, chain, c, p] for kind, chain in halves]) for p in range(2))
+        k = CAP * LAST.index(offset) + c
+        tiles[LATE + way * len(far) + k] = from_neighbour(way, NBR + k, own, grad_x, sides)
+
+    for kinds, offsets in (((0, 1), (-3, 3)), ((2,), (4,))):
+        for way in range(2):
+            @pl.when(there[1 - way])
+            def _(way=way):
+                for kind in kinds:
+                    for chain in range(2):
+                        late_copy(way, kind, chain).wait_recv()
+                for offset in offsets:
+                    for c in range(CAP):
+                        late_tile(way, offset, c)
+
+    def multiply(part, start):
         for k in range(4):
-            b = quarter * 4 + k
-            part[b] = jnp.dot(tiles[place_s[b]], weights[b], preferred_element_type=f32)
-
-    height = 16
-
-    @pl.loop(0, channels // height)
-    def _(strip):
-        here = pl.ds(pl.multiple_of(strip * height, height), height)
-        sums = [jnp.zeros((height, LANES), f32) for _ in range(OCN)]
-        for b in range(blocks):
-            value = part[b, here, :]
+            part[k] = jnp.dot(tiles[place_s[start + k]], weights[start + k], preferred_element_type=f32)
+
+    def add(part, start, live):
+        mine = [[((ocn_ref[start + k] == t) & live).astype(f32) for k in range(4)] for t in range(OCN)]
+        for strip in range(channels // 16):
+            here = pl.ds(16 * strip, 16)
+            values = [part[k, here, :] for k in range(4)]
             for t in range(OCN):
-                sums[t] = sums[t] + value * (ocn_ref[b] == t).astype(f32)
-        for t in range(OCN):
-            out_ref[here, t * LANES:(t + 1) * LANES] = sums[t].astype(bf16)
+                total = sums[t, here, :]
+                for k in range(4):
+                    total = total + values[k] * mine[t][k]
+                sums[t, here, :] = total
+
+    part_b[...] = jnp.zeros(part_b.shape, f32)
+    sums[...] = jnp.zeros(sums.shape, f32)
+
+    @pl.loop(0, blocks // 8)
+    def _(eight):
+        start = eight * 8
+        multiply(part_a, start)
+        add(part_b, jnp.maximum(start - 4, 0), eight > 0)
+        multiply(part_b, start + 4)
+        add(part_a, start, True)
+
+    add(part_b, blocks - 4, True)
+    for t in range(OCN):
+        out_ref[:, t * LANES:(t + 1) * LANES] = sums[t].astype(bf16)
 
     for way in range(2):
         for step in range(1, 4):
@@ -414,8 +453,9 @@
             for k in range(NBR):
                 near_copy(way, k).wait_send()
             fringe_copy(way).wait_send()
-            for chain in range(2):
-                late_copy(way, chain).wait_send()
+            for kind in range(3):
+                for chain in range(2):
+                    late_copy(way, kind, chain).wait_send()
 
 
 def solution(mesh):
@@ -455,11 +495,12 @@
                 pltpu.VMEM((2, CAP, 2, half, cells), bf16),
                 pltpu.VMEM((2, CAP, 2, half, cells), bf16),
                 pltpu.VMEM((2, CAP, 2, half, cells), bf16),
-                pltpu.VMEM((OWN, channels, 3 * cells), bf16),
+                pltpu.VMEM((2, CAP, 2, half, cells), bf16),
+                pltpu.VMEM((OWN, 2, channels, cells), bf16),
                 pltpu.VMEM((SLOTS, channels, 3 * cells), bf16),
                 pltpu.VMEM((2, NBR, 2, channels, cells), bf16),
                 pltpu.VMEM((2, NBR, 2, channels, cells), bf16),
-                pltpu.VMEM((2, 2, CAP, 2, half, cells), bf16),
+                pltpu.VMEM((2, 3, 2, CAP, 2, half, cells), bf16),
                 pltpu.VMEM((blocks, 3 * cells, cells), bf16),
                 pltpu.VMEM((channels * cx, cells), f32),
                 pltpu.VMEM((G, 8, LANES), i32),
@@ -468,8 +509,10 @@
                 pltpu.SMEM((2, 8, LANES), i32),
                 pltpu.SMEM((blocks,), i32),
                 pltpu.VMEM((2, LANES, LANES), bf16),
-                pltpu.VMEM((blocks, channels, cells), f32),
-                pltpu.VMEM((2, 16, channels), bf16),
+                pltpu.VMEM((4, channels, cells), f32),
+                pltpu.VMEM((4, channels, cells), f32),
+                pltpu.VMEM((OCN, channels, cells), f32),
+                pltpu.VMEM((2, 32, channels), bf16),
                 dma((2, 3, 4)), dma((2, 3, 4)),
                 dma((2, 2)), dma((2, 2)),
                 dma((2, 4)), dma((2, 4)),
@@ -478,7 +521,7 @@
                 dma((2,)), dma((2,)),
                 dma((2, NBR)), dma((2, NBR)),
                 dma((2,)), dma((2,)),
-                dma((2, 2)), dma((2, 2)),
+                dma((2, 3, 2)), dma((2, 3, 2)),
                 dma((G + 2,)),
                 dma((4,)),
                 dma,

time: 49.5 us -> 48.7 us (0.984)
  Pallas kernels: 48.7 us -> 47.9 us
    pallas_call x1, Pallas kernels: 48.7 us -> 47.9 us  [per_device(): pl.pallas_call(functools.partial(kernel, regions), out_shape=jax.ShapeDty...]
where the time goes in v3:
time: 48.7 us; the launch traced here: 48.5 us
  Pallas kernels  47.9 us (98%)
  local copies, waits for them, and re-layouts  0.66 us (1%)
    pallas_call x1, Pallas kernels, per_device(): pl.pallas_call(functools.partial(kernel, regions), out_shape=jax.ShapeDty...  47.9 us

profile of v3, /device:TPU:1, one launch (start us, length us, event | category | flops | bytes accessed | tf_op | source)
XLA Modules:
  0.0 48.5 jit_solution(9318983093910001789)
XLA Ops:
  0.0 47.9 %shard_map.55 = bf16[128,512]{1,0:T(8,128)(2,1)S(1)} custom-call(bf16[128,8,128]{2,1,0:T(8,128)(2,1)} %field_hbm.1, s32[16]{0:T(128)} %pick_hbm.1, s32[32]{0:T(128)} %src_hbm.1, s32[32]{0:T(128)} %ocn_hbm.1, bf16[32,384,128]{2,1,0:T(8,128)(2,1)} %w_hbm.1), custom_call_target="tpu_custom_call" | custom-call | flops 402653184 | bytes 4194304 | tf_op jit(solution)/shard_map/pallas_call | solution.py:473
  47.9 0.7 %copy.7 = bf16[128,512]{1,0:T(8,128)(2,1)} copy(bf16[128,512]{1,0:T(8,128)(2,1)S(1)} %shard_map.55) | data formatting | bytes 262144

commit v4 on v3

--- a/solution.py
+++ b/solution.py
@@ -14,7 +14,8 @@
 G = 8
 LANES = 128
 VMEM_LIMIT = 48 * 1024 * 1024
-ORDER = (0, 3, 1, 2)
+ORDER = (0, 7, 1, 2, 3, 4, 5, 6)
+DEPTH = 5
 OWN = G * CAP
 EARLY, LATE = OWN, OWN + 2 * NBR
 LAST = (-3, 3, 4)
@@ -119,10 +120,10 @@
 
     def ring(way, step, c):
         sign = -1 if way == 0 else 1
-        source = rows[sign * (step - 1)].at[pl.ds(2 * c, 2)]
+        source = rows[sign * (step - 1)].at[pl.ds(c, 1)]
         if step == 3:
-            source = rows[sign * 2].at[pl.ds(2 * c, 2), raw_half[way]]
-        return remote(source, rows[sign * step].at[pl.ds(2 * c, 2)],
+            source = rows[sign * 2].at[pl.ds(c, 1), raw_half[way]]
+        return remote(source, rows[sign * step].at[pl.ds(c, 1)],
                       ring_send.at[way, step - 1, c], ring_recv.at[way, step - 1, c], along(way))
 
     def passed(way, step):
@@ -182,12 +183,19 @@
             def _(way=way):
                 late_copy(way, kind, chain).start()
 
-    for c in ORDER:
-        for way in range(2):
-            ring(way, 1, c).start()
-        if c == 3:
-            for way in range(2):
-                send_halo(way, 0)
+    under_way = ([], [])
+
+    def send(way, copy):
+        if len(under_way[way]) == DEPTH:
+            under_way[way].pop(0).wait_send()
+        copy.start()
+        under_way[way].append(copy)
+
+    for way in range(2):
+        send_halo(way, 0)
+    for c in ORDER[:DEPTH]:
+        for way in range(2):
+            send(way, ring(way, 1, c))
 
     for copy in arriving[1:]:
         copy.wait()
@@ -208,6 +216,9 @@
         note_copy(way, 1).start()
         edge_copy(way, 1).start()
     to_smem(0).start()
+    for c in ORDER[DEPTH:]:
+        for way in range(2):
+            send(way, ring(way, 1, c))
 
     wanted = (distinct(src_ref, 0), distinct(src_ref, 2 * OWN))
     request = jnp.zeros((8, LANES), jnp.int32)
@@ -260,7 +271,7 @@
                 own, grad_x = raw_pair(offset, i, span)
                 target[way, c, 0] = own
                 target[way, c, 1] = grad_x
-            passed(way, step).start()
+            send(way, passed(way, step))
 
     def with_border(own, corners, prior, following):
         ends = (jnp.where((depth == following) & (column == LANES - 1), 0.5, 0.0)
@@ -281,11 +292,11 @@
             whole = jnp.concatenate([own, grad_x, grad_y], axis=1)
             tiles[CAP * h + c] = whole
 
+    def asked_to_smem(way):
+        return pltpu.make_async_copy(asked.at[1 - way], asked_s.at[1 - way], local_sem.at[G + way])
+
     def serve(way):
-        ask(1 - way).wait_recv()
-        to_scalar = pltpu.make_async_copy(asked.at[1 - way], asked_s.at[1 - way], local_sem.at[G + way])
-        to_scalar.start()
-        to_scalar.wait()
+        asked_to_smem(way).wait()
         for k in range(NBR):
             stage[way, k] = pairs[asked_s[1 - way, 0, way * NBR + k]]
             near_copy(way, k).start()
@@ -304,6 +315,22 @@
         fringe_copy(way).start()
 
     everything = pl.ds(0, channels)
+
+    def early_tiles():
+        for offset in (0, -1, 1):
+            halos_arrived(offset)
+            to_smem(offset).wait()
+        for offset in (0, -1, 1, -2, 2):
+            for c in range(CAP):
+                h = at(offset)
+                own, grad_x = raw_pair(offset, picked(h, me, c), everything)
+                pairs[CAP * h + c, 0] = own
+                pairs[CAP * h + c, 1] = grad_x
+        for way in range(2):
+            @pl.when(there[way])
+            def _(way=way):
+                serve(way)
+
     for step in range(1, 5):
         ways = (0, 1) if step < 4 else (0,)
         for way in ways:
@@ -315,35 +342,29 @@
             to_smem(-step if way == 0 else step).start()
         if step == 4:
             break
+        if step == 2:
+            for way in range(2):
+                @pl.when(there[way])
+                def _(way=way):
+                    ask(1 - way).wait_recv()
+                    asked_to_smem(way).start()
         for c in ORDER:
+            if step == 3 and c == ORDER[2]:
+                early_tiles()
             for way in range(2):
                 ring(way, step, c).wait_recv()
                 if step < 3:
-                    ring(way, step + 1, c).start()
+                    send(way, ring(way, step + 1, c))
                 offset = -step if way == 0 else step
                 if c == 0:
                     send_halo(1, offset)
-                if c == 3:
+                if c == 7:
                     send_halo(0, offset)
         if step >= 2:
             for offset in (-step, step):
                 halos_arrived(offset)
                 to_smem(offset).wait()
             pass_on(step + 1)
-        if step == 2:
-            for offset in (0, -1, 1):
-                halos_arrived(offset)
-                to_smem(offset).wait()
-            for offset in (0, -1, 1, -2, 2):
-                for c in range(CAP):
-                    h = at(offset)
-                    own, grad_x = raw_pair(offset, picked(h, me, c), everything)
-                    pairs[CAP * h + c, 0] = own
-                    pairs[CAP * h + c, 1] = grad_x
-            for way in range(2):
-                @pl.when(there[way])
-                def _(way=way):
-                    serve(way)
         if step == 3:
             for way, offset in ((0, -3), (1, 3)):
                 for c in range(CAP):
@@ -436,11 +457,8 @@
         out_ref[:, t * LANES:(t + 1) * LANES] = sums[t].astype(bf16)
 
     for way in range(2):
-        for step in range(1, 4):
-            for c in ORDER:
-                ring(way, step, c).wait_send()
-        for step in (3, 4):
-            passed(way, step).wait_send()
+        for copy in under_way[way]:
+            copy.wait_send()
         for step in range(1, 5 - way):
             note_copy(way, step).wait_send()
             edge_copy(way, step).wait_send()
@@ -513,7 +531,7 @@
                 pltpu.VMEM((4, channels, cells), f32),
                 pltpu.VMEM((OCN, channels, cells), f32),
                 pltpu.VMEM((2, 32, channels), bf16),
-                dma((2, 3, 4)), dma((2, 3, 4)),
+                dma((2, 3, 8)), dma((2, 3, 8)),
                 dma((2, 2)), dma((2, 2)),
                 dma((2, 4)), dma((2, 4)),
                 dma((2, 4)), dma((2, 4)),

time: 48.7 us -> 43.3 us (0.89)
  Pallas kernels: 47.9 us -> 42.5 us
    pallas_call x1, Pallas kernels: 47.9 us -> 42.5 us  [per_device(): pl.pallas_call(functools.partial(kernel, regions), out_shape=jax.ShapeDty...]
where the time goes in v4:
time: 43.3 us; the launch traced here: 43.1 us
  Pallas kernels  42.5 us (98%)
  local copies, waits for them, and re-layouts  0.66 us (2%)
    pallas_call x1, Pallas kernels, per_device(): pl.pallas_call(functools.partial(kernel, regions), out_shape=jax.ShapeDty...  42.5 us

profile of v4, /device:TPU:1, one launch (start us, length us, event | category | flops | bytes accessed | tf_op | source)
XLA Modules:
  0.0 43.1 jit_solution(17306238612762911208)
XLA Ops:
  0.0 42.5 %shard_map.55 = bf16[128,512]{1,0:T(8,128)(2,1)S(1)} custom-call(bf16[128,8,128]{2,1,0:T(8,128)(2,1)} %field_hbm.1, s32[16]{0:T(128)} %pick_hbm.1, s32[32]{0:T(128)} %src_hbm.1, s32[32]{0:T(128)} %ocn_hbm.1, bf16[32,384,128]{2,1,0:T(8,128)(2,1)} %w_hbm.1), custom_call_target="tpu_custom_call" | custom-call | flops 402653184 | bytes 4194304 | tf_op jit(solution)/shard_map/pallas_call | solution.py:491
  42.5 0.7 %copy.7 = bf16[128,512]{1,0:T(8,128)(2,1)} copy(bf16[128,512]{1,0:T(8,128)(2,1)S(1)} %shard_map.55) | data formatting | bytes 262144

commit v5 on v4

--- a/solution.py
+++ b/solution.py
@@ -126,10 +126,10 @@
         return remote(source, rows[sign * step].at[pl.ds(c, 1)],
                       ring_send.at[way, step - 1, c], ring_recv.at[way, step - 1, c], along(way))
 
-    def passed(way, step):
+    def passed(way, step, c):
         source, target = (pass3, got3) if step == 3 else (pass4, got4)
-        return remote(source.at[way], target.at[way],
-                      pass_send.at[way, step - 3], pass_recv.at[way, step - 3], along(way))
+        return remote(source.at[way, c], target.at[way, c],
+                      pass_send.at[way, step - 3, c], pass_recv.at[way, step - 3, c], along(way))
 
     def note_copy(way, step, receiving=False):
         sign = -1 if way == 0 else 1
@@ -173,15 +173,15 @@
         return remote(fringe_out.at[way], fringe.at[pl.ds(32 * way, 32)],
                       fringe_send.at[way], fringe_recv.at[way], across(way))
 
-    def late_copy(way, kind, chain):
-        return remote((raw3, got3, got4)[kind].at[chain], late.at[way, kind, chain],
-                      late_send.at[way, kind, chain], late_recv.at[way, kind, chain], across(way))
-
-    def send_late(kind, chain):
+    def late_copy(way, kind, chain, c):
+        return remote((raw3, got3, got4)[kind].at[chain, c], late.at[way, kind, chain, c],
+                      late_send.at[way, kind, chain, c], late_recv.at[way, kind, chain, c], across(way))
+
+    def send_late(kind, chain, c):
         for way in range(2):
             @pl.when(there[way])
             def _(way=way):
-                late_copy(way, kind, chain).start()
+                late_copy(way, kind, chain, c).start()
 
     under_way = ([], [])
 
@@ -262,16 +262,15 @@
         return own, ((down - up) * 0.5).astype(bf16)
 
     def pass_on(step):
-        for way in range(2):
-            offset = -(step - 1) if way == 0 else step - 1
-            span = raw_half[1 - way] if step == 3 else raw_half[way]
-            target = pass3 if step == 3 else pass4
-            for c in range(CAP):
-                i = picked(at(offset), along(way)[0], c)
-                own, grad_x = raw_pair(offset, i, span)
+        for c in range(CAP):
+            for way in range(2):
+                offset = -(step - 1) if way == 0 else step - 1
+                span = raw_half[1 - way] if step == 3 else raw_half[way]
+                target = pass3 if step == 3 else pass4
+                own, grad_x = raw_pair(offset, picked(at(offset), along(way)[0], c), span)
                 target[way, c, 0] = own
                 target[way, c, 1] = grad_x
-            send(way, passed(way, step))
+                send(way, passed(way, step, c))
 
     def with_border(own, corners, prior, following):
         ends = (jnp.where((depth == following) & (column == LANES - 1), 0.5, 0.0)
@@ -371,12 +370,13 @@
                     own, grad_x = raw_pair(offset, picked(at(offset), me, c), raw_half[way])
                     raw3[way, c, 0] = own
                     raw3[way, c, 1] = grad_x
-                send_late(0, way)
+                    send_late(0, way, c)
 
     to_smem(-4).wait()
-    for chain in range(2):
-        passed(chain, 3).wait_recv()
-        send_late(1, chain)
+    for c in range(CAP):
+        for chain in range(2):
+            passed(chain, 3, c).wait_recv()
+            send_late(1, chain, c)
     for way in range(2):
         @pl.when(there[way])
         def _(way=way):
@@ -386,9 +386,10 @@
         keep(offset, lambda h, c: (pairs[CAP * h + c, 0], pairs[CAP * h + c, 1]), corners)
     keep(-3, lambda h, c: tuple(joined(raw3[0, c, p], got3[0, c, p]) for p in range(2)), corners)
     keep(3, lambda h, c: tuple(joined(got3[1, c, p], raw3[1, c, p]) for p in range(2)), corners)
-    for chain in range(2):
-        passed(chain, 4).wait_recv()
-        send_late(2, chain)
+    for c in range(CAP):
+        for chain in range(2):
+            passed(chain, 4, c).wait_recv()
+            send_late(2, chain, c)
     keep(4, lambda h, c: tuple(joined(got4[0, c, p], got4[1, c, p]) for p in range(2)), corners)
 
     def from_neighbour(way, k, own, grad_x, sides):
@@ -421,7 +422,8 @@
             def _(way=way):
                 for kind in kinds:
                     for chain in range(2):
-                        late_copy(way, kind, chain).wait_recv()
+                        for c in range(CAP):
+                            late_copy(way, kind, chain, c).wait_recv()
                 for offset in offsets:
                     for c in range(CAP):
                         late_tile(way, offset, c)
@@ -444,11 +446,10 @@
     part_b[...] = jnp.zeros(part_b.shape, f32)
     sums[...] = jnp.zeros(sums.shape, f32)
 
-    @pl.loop(0, blocks // 8)
-    def _(eight):
-        start = eight * 8
+    for start in range(0, blocks, 8):
         multiply(part_a, start)
-        add(part_b, jnp.maximum(start - 4, 0), eight > 0)
+        if start > 0:
+            add(part_b, start - 4, True)
         multiply(part_b, start + 4)
         add(part_a, start, True)
 
@@ -473,7 +474,8 @@
             fringe_copy(way).wait_send()
             for kind in range(3):
                 for chain in range(2):
-                    late_copy(way, kind, chain).wait_send()
+                    for c in range(CAP):
+                        late_copy(way, kind, chain, c).wait_send()
 
 
 def solution(mesh):
@@ -532,14 +534,14 @@
                 pltpu.VMEM((OCN, channels, cells), f32),
                 pltpu.VMEM((2, 32, channels), bf16),
                 dma((2, 3, 8)), dma((2, 3, 8)),
-                dma((2, 2)), dma((2, 2)),
+                dma((2, 2, CAP)), dma((2, 2, CAP)),
                 dma((2, 4)), dma((2, 4)),
                 dma((2, 4)), dma((2, 4)),
                 dma((2, G)), dma((2, G)),
                 dma((2,)), dma((2,)),
                 dma((2, NBR)), dma((2, NBR)),
                 dma((2,)), dma((2,)),
-                dma((2, 3, 2)), dma((2, 3, 2)),
+                dma((2, 3, 2, CAP)), dma((2, 3, 2, CAP)),
                 dma((G + 2,)),
                 dma((4,)),
                 dma,

time: 43.3 us -> 42.7 us (0.986)
  Pallas kernels: 42.5 us -> 41.9 us
    pallas_call x1, Pallas kernels: 42.5 us -> 41.9 us  [per_device(): pl.pallas_call(functools.partial(kernel, regions), out_shape=jax.ShapeDty...]
where the time goes in v5:
time: 42.7 us; the launch traced here: 42.5 us
  Pallas kernels  41.9 us (98%)
  local copies, waits for them, and re-layouts  0.66 us (2%)
    pallas_call x1, Pallas kernels, per_device(): pl.pallas_call(functools.partial(kernel, regions), out_shape=jax.ShapeDty...  41.9 us

profile of v5, /device:TPU:1, one launch (start us, length us, event | category | flops | bytes accessed | tf_op | source)
XLA Modules:
  0.0 42.5 jit_solution(1041748297175605092)
XLA Ops:
  0.0 41.9 %shard_map.55 = bf16[128,512]{1,0:T(8,128)(2,1)S(1)} custom-call(bf16[128,8,128]{2,1,0:T(8,128)(2,1)} %field_hbm.1, s32[16]{0:T(128)} %pick_hbm.1, s32[32]{0:T(128)} %src_hbm.1, s32[32]{0:T(128)} %ocn_hbm.1, bf16[32,384,128]{2,1,0:T(8,128)(2,1)} %w_hbm.1), custom_call_target="tpu_custom_call" | custom-call | flops 402653184 | bytes 4194304 | tf_op jit(solution)/shard_map/pallas_call | solution.py:493
  41.9 0.7 %copy.7 = bf16[128,512]{1,0:T(8,128)(2,1)} copy(bf16[128,512]{1,0:T(8,128)(2,1)S(1)} %shard_map.55) | data formatting | bytes 262144
